TPU v7x, 32 devices: a whole 2x2x4 slice. The times are simulated.
32 devices in a mesh: layer: 8 (over y, x, core), tp: 4 (over z).
Axes of the slice: x: 2, y: 2, z: 4, core: 2. Of those that a mesh axis runs over, the one named last changes fastest.
Arguments:
- acts: bfloat16 [1024, 2048], P(('layer', 'tp')), may hold values from -12 to 12, as said below
- fresh: bfloat16 [2, 128, 2048], P(None, 'tp'), may hold values from -12 to 12, as said below
- norm_first: float32 [4, 2048], replicated, may hold values from 0.5 to 1.5
- norm_second: float32 [4, 2048], replicated, may hold values from 0.5 to 1.5
- proj_qkv: bfloat16 [32, 2048, 192], P(('layer', 'tp')), may hold values from -1 to 1
- proj_out: bfloat16 [2048, 2048], P(('layer', 'tp')), may hold values from -0.25 to 0.25
- proj_gate_up: bfloat16 [2048, 2, 8192], P(None, None, ('layer', 'tp')), may hold values from -0.125 to 0.125
- proj_down: bfloat16 [8192, 2048], P(('layer', 'tp')), may hold values from -0.125 to 0.125
- memory_state: float32 [32, 64, 64], P(('layer', 'tp')), may hold values from -768 to 768
- memory_norm: float32 [32, 64], P(('layer', 'tp')), may hold values from 16 to 256
- bias_gate: float32 [32], P(('layer', 'tp')), may hold values from -3 to 3
Outputs:
- first_out: bfloat16 [1024, 2048], P(('layer', 'tp'))
- second_out: bfloat16 [1024, 2048], P(('layer', 'tp'))
- memory_after: float32 [32, 64, 64], P(('layer', 'tp'))
- norm_after: float32 [32, 64], P(('layer', 'tp'))
Inputs may be any that keep to these rules, and one draw needn't show every extreme that they name: `acts`: activation rows. `fresh`: activation rows.
All inputs are finite; a program needn't handle non-finite values.
Results may differ from a plain program's by a relative error of at most 0.025.
Values may be sent and summed in bfloat16 or wider, within the bound.
A program may use at most 64 MiB of HBM per device.

v0:
```python
import jax
import jax.numpy as jnp
from jax import lax
from jax.sharding import PartitionSpec as P


def partner_2(value, axis, distance):
    mask = 2**distance
    pairs = [(source, source ^ mask) for source in range(lax.axis_size(axis))]
    return lax.ppermute(value, axis, pairs)


def shifted(value, axis, steps):
    count = lax.axis_size(axis)
    initial, last = (max(0, -steps), min(count, count - steps))
    return lax.ppermute(value, axis, [(source, source + steps) for source in range(initial, last)])


def rms_norm(values, weight):
    floats = values.astype(jnp.float32)
    scaled = floats * lax.rsqrt(jnp.mean(floats * floats, axis=-1, keepdims=True) + 1e-05)
    return (scaled * weight).astype(jnp.bfloat16)


def attend(qkv, memory, totals, logits):
    head_dim = memory.shape[-1]
    seg_len = qkv.shape[0]
    queries = qkv[..., :head_dim]
    keyed = qkv[..., head_dim : 2 * head_dim]
    valued = qkv[..., 2 * head_dim :]
    scores = jnp.einsum(
        "qhc,khc->hqk", queries, keyed, preferred_element_type=jnp.float32
    ) * head_dim ** (-0.5)
    positions = jnp.arange(seg_len)
    allowed = positions[:, None] >= positions[None, :]
    probs = jax.nn.softmax(jnp.where(allowed[None], scores, -jnp.inf), axis=-1).astype(jnp.bfloat16)
    direct = jnp.einsum("hqk,khc->qhc", probs, valued, preferred_element_type=jnp.float32)
    lifted_q = jax.nn.elu(queries.astype(jnp.float32)) + 1.0
    lifted_k = jax.nn.elu(keyed.astype(jnp.float32)) + 1.0
    numer = jnp.einsum("qhc,hce->qhe", lifted_q, memory, precision=lax.Precision.HIGHEST)
    denom = jnp.einsum("qhc,hc->qh", lifted_q, totals, precision=lax.Precision.HIGHEST)[..., None]
    gate_open = jax.nn.sigmoid(logits)[None, :, None]
    blended = (gate_open * numer / denom + (1.0 - gate_open) * direct).astype(jnp.bfloat16)
    new_memory = memory + jnp.einsum(
        "khc,khe->hce", lifted_k, valued.astype(jnp.float32), precision=lax.Precision.HIGHEST
    )
    new_totals = totals + jnp.sum(lifted_k, axis=0)
    return (blended.reshape(seg_len, -1), new_memory, new_totals)


def body(
    acts,
    fresh,
    norm_first,
    norm_second,
    proj_qkv,
    proj_out,
    proj_gate_up,
    proj_down,
    memory_state,
    memory_norm,
    bias_gate,
):
    position = lax.axis_index("layer")
    lower = position % 2 == 0
    depth = position // 2
    group = lax.axis_size("tp")
    gain_one = lax.dynamic_index_in_dim(norm_first, depth, 0, keepdims=False)
    gain_two = lax.dynamic_index_in_dim(norm_second, depth, 0, keepdims=False)
    row_count = acts.shape[0]

    def ordered(mine, other):
        return jnp.concatenate(
            [jnp.where(lower, mine, other), jnp.where(lower, other, mine)], axis=0
        )

    def project(rows):
        return jnp.einsum("sd,hdc->shc", rows, proj_qkv, preferred_element_type=jnp.float32).astype(
            jnp.bfloat16
        )

    def expand(rows):
        gate_up = jnp.einsum("sd,dtf->stf", rows, proj_gate_up, preferred_element_type=jnp.float32)
        return (jax.nn.silu(gate_up[:, 0]) * gate_up[:, 1]).astype(jnp.bfloat16)

    def collect_rows(values):
        partner = partner_2(values, "layer", 0)
        mine, other = (
            lax.all_gather(values, "tp", axis=0, tiled=True),
            lax.all_gather(partner, "tp", axis=0, tiled=True),
        )
        return ordered(mine, other)

    def reduce_rows(local, weight):
        seg_len = local.shape[0]
        columns = local.shape[1]
        domain = jnp.transpose(local.reshape(2, group, row_count, columns), (1, 0, 2, 3)).reshape(
            seg_len, columns
        )
        both = lax.psum_scatter(
            jnp.dot(domain, weight, preferred_element_type=jnp.float32).astype(jnp.bfloat16),
            "tp",
            scatter_dimension=0,
            tiled=True,
        ).astype(jnp.float32)
        kept = jnp.where(lower, both[:row_count], both[row_count:])
        given = jnp.where(lower, both[row_count:], both[:row_count])
        return kept + partner_2(given.astype(jnp.bfloat16), "layer", 0).astype(given.dtype)

    def apply_layer(stream, memory, totals):
        qkv = project(collect_rows(rms_norm(stream, gain_one)))
        blended, memory, totals = attend(qkv, memory, totals, bias_gate)
        attn = reduce_rows(blended, proj_out)
        hidden_one = (stream.astype(jnp.float32) + attn).astype(jnp.bfloat16)
        hidden = expand(collect_rows(rms_norm(hidden_one, gain_two)))
        ffn = reduce_rows(hidden, proj_down)
        output = (hidden_one.astype(jnp.float32) + ffn).astype(jnp.bfloat16)
        return (output, memory, totals)

    first_rows, memory_one, totals_one = apply_layer(acts, memory_state, memory_norm)
    incoming = shifted(first_rows, "layer", 2)
    fresh_rows = lax.dynamic_index_in_dim(fresh, position % 2, 0, keepdims=False)
    entering = jnp.where(depth == 0, fresh_rows, incoming)
    second_rows, memory_two, totals_two = apply_layer(entering, memory_one, totals_one)
    return (first_rows, second_rows, memory_two, totals_two)


def solution(mesh):
    in_specs = (
        P(("layer", "tp"), None),
        P(None, "tp", None),
        P(),
        P(),
        P(("layer", "tp"), None, None),
        P(("layer", "tp"), None),
        P(None, None, ("layer", "tp")),
        P(("layer", "tp"), None),
        P(("layer", "tp"), None, None),
        P(("layer", "tp"), None),
        P(("layer", "tp")),
    )
    out_specs = (
        P(("layer", "tp"), None),
        P(("layer", "tp"), None),
        P(("layer", "tp"), None, None),
        P(("layer", "tp"), None),
    )
    return jax.shard_map(body, mesh=mesh, in_specs=in_specs, out_specs=out_specs, check_vma=False)
```

profile of v0, /device:TPU:0, one launch (start us, length us, event | category | flops | bytes accessed | tf_op | source)
XLA Modules:
  0.0 291.3 jit_solution(13810970095336967738)
XLA Ops:
  7.3 1.2 fusion.34
  8.5 0.8 constant_dynamic-slice_fusion.1
  9.3 1.0 fusion.36
  10.3 0.5 collective-permute-start
  11.5 17.5 %all_gather.24 = bf16[128,2048]{1,0:T(8,128)(2,1)S(1)} all-gather(bf16[32,2048]{1,0:T(8,128)(2,1)S(1)} %fusion.36), channel_id=1, replica_groups=mesh['layer'=8,'tp'=4] {'tp'}, dimensions={0}, use_global_device_ids=true | all-gather | bytes 655360 | tf_op jit(solution)/shard_map/all_gather | solution.py:89
  29.1 15.5 %all_gather.25 = bf16[128,2048]{1,0:T(8,128)(2,1)S(1)} all-gather(bf16[32,2048]{1,0:T(8,128)(2,1)S(1)} %collective-permute-done), channel_id=1, replica_groups=mesh['layer'=8,'tp'=4] {'tp'}, dimensions={0}, use_global_device_ids=true | all-gather | bytes 655360 | tf_op jit(solution)/shard_map/all_gather | solution.py:90
  44.7 0.5 fusion.6
  45.2 0.3 fusion.126
  45.5 0.2 fusion.73
  45.7 0.3 fusion.20
  46.0 0.2 fusion.17
  46.2 0.1 copy.17
  46.3 1.4 convolution_convert_fusion.3
  47.8 28.7 %reduce-scatter.5.cloned.1.call-done = bf16[64,2048]{1,0:T(8,128)(2,1)} async-done(((bf16[256,2048]{1,0:T(8,128)(2,1)}), bf16[64,2048]{1,0:T(8,128)(2,1)}) %reduce-scatter.5.cloned.1.call-update) | async-done | bytes 262160 | tf_op jit(solution)/shard_map/reduce_scatter | solution.py:100
  76.5 1.0 convert_element_type.151
  77.6 0.8 constant_dynamic-slice_fusion
  78.3 0.6 collective-permute-done.1
  78.9 0.2 fusion.38
  79.1 0.1 fusion.40
  79.2 0.2 collective-permute-start.2
  79.4 16.2 %all_gather.26 = bf16[128,2048]{1,0:T(8,128)(2,1)S(1)} all-gather(bf16[32,2048]{1,0:T(8,128)(2,1)S(1)} %fusion.40), channel_id=1, replica_groups=mesh['layer'=8,'tp'=4] {'tp'}, dimensions={0}, use_global_device_ids=true | all-gather | bytes 655360 | tf_op jit(solution)/shard_map/all_gather | solution.py:89
  95.7 14.7 %all_gather.27 = bf16[128,2048]{1,0:T(8,128)(2,1)S(1)} all-gather(bf16[32,2048]{1,0:T(8,128)(2,1)S(1)} %collective-permute-done.2), channel_id=1, replica_groups=mesh['layer'=8,'tp'=4] {'tp'}, dimensions={0}, use_global_device_ids=true | all-gather | bytes 655360 | tf_op jit(solution)/shard_map/all_gather | solution.py:90
  110.4 0.7 fusion.2
  111.3 1.1 copy-done.1
  112.4 1.4 convolution_convert_fusion.1
  113.8 27.0 %reduce-scatter.7.cloned.1.call-done = bf16[64,2048]{1,0:T(8,128)(2,1)} async-done(((bf16[256,2048]{1,0:T(8,128)(2,1)}), bf16[64,2048]{1,0:T(8,128)(2,1)}) %reduce-scatter.7.cloned.1.call-update) | async-done | bytes 262160 | tf_op jit(solution)/shard_map/reduce_scatter | solution.py:100
  140.8 1.0 convert_element_type.159
  141.8 0.8 copy-done.2
  142.6 0.7 select_convert_fusion.2
  143.3 1.7 collective-permute-done.3
  145.0 1.1 fusion.41
  146.1 3.4 %collective-permute-start.4 = (bf16[32,2048]{1,0:T(8,128)(2,1)S(1)}, bf16[32,2048]{1,0:T(8,128)(2,1)S(1)}, u32[]{:S(2)}, u32[]{:S(2)}) collective-permute-start(bf16[32,2048]{1,0:T(8,128)(2,1)S(1)} %fusion.41), channel_id=1, source_target_pairs={{0,8},{4,12},{8,16},{12,20},{16,24},{20,28},{1,9},{5,13},{9,17},{1... | collective-permute-start | bytes 393224 | tf_op jit(solution)/shard_map/ppermute | solution.py:16
  149.5 1.0 fusion.18
  150.5 1.0 fusion.71
  151.5 1.1 collective-permute-done.4
  152.6 1.1 fusion.42
  153.6 0.1 fusion.44
  153.8 16.1 %all_gather.28 = bf16[128,2048]{1,0:T(8,128)(2,1)S(1)} all-gather(bf16[32,2048]{1,0:T(8,128)(2,1)S(1)} %fusion.44), channel_id=1, replica_groups=mesh['layer'=8,'tp'=4] {'tp'}, dimensions={0}, use_global_device_ids=true | all-gather | bytes 655360 | tf_op jit(solution)/shard_map/all_gather | solution.py:89
  170.0 15.7 %all_gather.29 = bf16[128,2048]{1,0:T(8,128)(2,1)S(1)} all-gather(bf16[32,2048]{1,0:T(8,128)(2,1)S(1)} %collective-permute-done.5), channel_id=1, replica_groups=mesh['layer'=8,'tp'=4] {'tp'}, dimensions={0}, use_global_device_ids=true | all-gather | bytes 655360 | tf_op jit(solution)/shard_map/all_gather | solution.py:90
  185.8 0.5 fusion.7
  186.4 0.3 fusion.127
  186.6 0.2 fusion.68
  186.8 0.3 fusion.21
  187.2 0.8 fusion.16
  188.0 1.5 copy.23
  189.4 0.8 copy.24
  190.3 1.4 convolution_convert_fusion.2
  191.7 26.6 %reduce-scatter.9.cloned.1.call-done = bf16[64,2048]{1,0:T(8,128)(2,1)} async-done(((bf16[256,2048]{1,0:T(8,128)(2,1)}), bf16[64,2048]{1,0:T(8,128)(2,1)}) %reduce-scatter.9.cloned.1.call-update) | async-done | bytes 262160 | tf_op jit(solution)/shard_map/reduce_scatter | solution.py:100
  218.3 1.0 convert_element_type.173
  219.4 1.3 collective-permute-done.6
  220.7 0.2 fusion.46
  220.9 0.1 fusion.48
  221.1 0.2 collective-permute-start.7
  221.3 16.2 %all_gather.30 = bf16[128,2048]{1,0:T(8,128)(2,1)S(1)} all-gather(bf16[32,2048]{1,0:T(8,128)(2,1)S(1)} %fusion.48), channel_id=1, replica_groups=mesh['layer'=8,'tp'=4] {'tp'}, dimensions={0}, use_global_device_ids=true | all-gather | bytes 655360 | tf_op jit(solution)/shard_map/all_gather | solution.py:89
  237.5 14.7 %all_gather.31 = bf16[128,2048]{1,0:T(8,128)(2,1)S(1)} all-gather(bf16[32,2048]{1,0:T(8,128)(2,1)S(1)} %collective-permute-done.7), channel_id=1, replica_groups=mesh['layer'=8,'tp'=4] {'tp'}, dimensions={0}, use_global_device_ids=true | all-gather | bytes 655360 | tf_op jit(solution)/shard_map/all_gather | solution.py:90
  252.3 0.7 fusion
  253.2 1.4 convolution_convert_fusion
  254.6 0.1 fusion.66
  254.7 0.8 fusion.19
  255.6 26.0 %reduce-scatter.11.cloned.1.call-done = bf16[64,2048]{1,0:T(8,128)(2,1)} async-done(((bf16[256,2048]{1,0:T(8,128)(2,1)}), bf16[64,2048]{1,0:T(8,128)(2,1)}) %reduce-scatter.11.cloned.1.call-update) | async-done | bytes 262160 | tf_op jit(solution)/shard_map/reduce_scatter | solution.py:100
  281.6 1.0 convert_element_type.181
  282.7 0.5 bitcast_add_fusion
  283.2 0.8 collective-permute-done.8
  284.0 0.7 fusion.49
  (71 shorter events, 1.4 us)
Async XLA Ops:
  7.2 103.3 %copy-start = (bf16[2048,2,256]{2,1,0:T(2,128)(2,1)S(1)}, bf16[2048,2,256]{2,1,0:T(2,128)(2,1)}, u32[]{:S(2)}) copy-start(bf16[2048,2,256]{2,1,0:T(2,128)(2,1)} %param.17) | copy-start | bytes 6291460
  7.2 37.5 %copy-start.14 = (bf16[1,2048,192]{1,2,0:T(8,128)(2,1)S(1)}, bf16[1,2048,192]{1,2,0:T(8,128)(2,1)}, u32[]{:S(2)}) copy-start(bf16[1,2048,192]{1,2,0:T(8,128)(2,1)} %param.15) | copy-start | bytes 2359300
  7.2 69.3 %reduce-scatter.5.cloned.1.call-start = ((), (), s32[]{:S(2)}) async-start(), calls=%async_computation.4 | async-start | bytes 1310720 | tf_op jit(solution)/shard_map/reduce_scatter | solution.py:100
  10.3 18.8 %collective-permute-start = (bf16[32,2048]{1,0:T(8,128)(2,1)S(1)}, bf16[32,2048]{1,0:T(8,128)(2,1)S(1)}, u32[]{:S(2)}, u32[]{:S(2)}) collective-permute-start(bf16[32,2048]{1,0:T(8,128)(2,1)S(1)} %fusion.36), channel_id=1, source_target_pairs={{0,4},{4,0},{8,12},{12,8},{16,20},{20,16},{24,28},{28,24},{1,5},{5... | collective-permute-start | bytes 393224 | tf_op jit(solution)/shard_map/ppermute | solution.py:10
  44.6 0.8 copy-start.11
  44.7 1.1 copy-start.16
  44.7 1.6 copy-start.4
  45.2 0.8 copy-start.6
  46.2 32.7 %copy-start.3 = (bf16[32,2048]{1,0:T(8,128)(2,1)S(1)}, bf16[32,2048]{1,0:T(8,128)(2,1)}, u32[]{:S(2)}) copy-start(bf16[32,2048]{1,0:T(8,128)(2,1)} %param.11) | copy-start | bytes 393220
  47.7 93.1 %reduce-scatter.7.cloned.1.call-start = ((), (), s32[]{:S(2)}) async-start(), calls=%async_computation.5 | async-start | bytes 1310720 | tf_op jit(solution)/shard_map/reduce_scatter | solution.py:100
  77.5 1.4 collective-permute-start.1
  79.2 16.5 %collective-permute-start.2 = (bf16[32,2048]{1,0:T(8,128)(2,1)S(1)}, bf16[32,2048]{1,0:T(8,128)(2,1)S(1)}, u32[]{:S(2)}, u32[]{:S(2)}) collective-permute-start(bf16[32,2048]{1,0:T(8,128)(2,1)S(1)} %fusion.40), channel_id=1, source_target_pairs={{0,4},{4,0},{8,12},{12,8},{16,20},{20,16},{24,28},{28,24},{1,5},{5... | collective-permute-start | bytes 393224 | tf_op jit(solution)/shard_map/ppermute | solution.py:10
  111.1 1.2 copy-start.1
  113.8 104.5 %reduce-scatter.9.cloned.1.call-start = ((), (), s32[]{:S(2)}) async-start(), calls=%async_computation.6 | async-start | bytes 1310720 | tf_op jit(solution)/shard_map/reduce_scatter | solution.py:100
  141.8 0.8 copy-start.2
  143.3 1.7 collective-permute-start.3
  146.1 23.9 %copy-start.5 = (bf16[32,2048]{1,0:T(8,128)(2,1)}, bf16[32,2048]{1,0:T(8,128)(2,1)S(1)}, u32[]{:S(2)}) copy-start(bf16[32,2048]{1,0:T(8,128)(2,1)S(1)} %fusion.41) | copy-start | bytes 393220
  146.1 6.4 %collective-permute-start.4 = (bf16[32,2048]{1,0:T(8,128)(2,1)S(1)}, bf16[32,2048]{1,0:T(8,128)(2,1)S(1)}, u32[]{:S(2)}, u32[]{:S(2)}) collective-permute-start(bf16[32,2048]{1,0:T(8,128)(2,1)S(1)} %fusion.41), channel_id=1, source_target_pairs={{0,8},{4,12},{8,16},{12,20},{16,24},{20,28},{1,9},{5,13},{9,17},{1... | collective-permute-start | bytes 393224 | tf_op jit(solution)/shard_map/ppermute | solution.py:16
  150.5 36.3 %copy-start.17 = (f32[1,64,64]{2,1,0:T(8,128)}, f32[1,64,64]{2,1,0:T(8,128)S(1)}, u32[]{:S(2)}) copy-start(f32[1,64,64]{2,1,0:T(8,128)S(1)} %fusion.18) | copy-start | bytes 49156
  150.5 35.3 %copy-start.15 = (bf16[1,2048,192]{1,2,0:T(8,128)(2,1)S(1)}, bf16[1,2048,192]{1,2,0:T(8,128)(2,1)}, u32[]{:S(2)}) copy-start(bf16[1,2048,192]{1,2,0:T(8,128)(2,1)} %param.15) | copy-start | bytes 2359300
  151.5 35.1 %copy-start.9 = (f32[64]{0:T(128)}, f32[64]{0:T(128)S(1)}, u32[]{:S(2)}) copy-start(f32[64]{0:T(128)S(1)} %fusion.71) | copy-start | bytes 772
  153.8 16.2 %collective-permute-start.5 = (bf16[32,2048]{1,0:T(8,128)(2,1)S(1)}, bf16[32,2048]{1,0:T(8,128)(2,1)S(1)}, u32[]{:S(2)}, u32[]{:S(2)}) collective-permute-start(bf16[32,2048]{1,0:T(8,128)(2,1)S(1)} %fusion.44), channel_id=1, source_target_pairs={{0,4},{4,0},{8,12},{12,8},{16,20},{20,16},{24,28},{28,24},{1,5},{5... | collective-permute-start | bytes 393224 | tf_op jit(solution)/shard_map/ppermute | solution.py:10
  185.8 0.8 copy-start.12
  186.4 0.8 copy-start.7
  191.7 89.9 %reduce-scatter.11.cloned.1.call-start = ((), (), s32[]{:S(2)}) async-start(), calls=%async_computation.7 | async-start | bytes 1310720 | tf_op jit(solution)/shard_map/reduce_scatter | solution.py:100
  219.3 1.4 collective-permute-start.6
  221.1 16.5 %collective-permute-start.7 = (bf16[32,2048]{1,0:T(8,128)(2,1)S(1)}, bf16[32,2048]{1,0:T(8,128)(2,1)S(1)}, u32[]{:S(2)}, u32[]{:S(2)}) collective-permute-start(bf16[32,2048]{1,0:T(8,128)(2,1)S(1)} %fusion.48), channel_id=1, source_target_pairs={{0,4},{4,0},{8,12},{12,8},{16,20},{20,16},{24,28},{28,24},{1,5},{5... | collective-permute-start | bytes 393224 | tf_op jit(solution)/shard_map/ppermute | solution.py:10
  253.0 1.6 copy-start.8
  253.0 1.7 copy-start.18
  253.1 29.5 %copy-start.10 = (f32[64]{0:T(128)S(1)}, f32[64]{0:T(128)}, u32[]{:S(2)}) copy-start(f32[64]{0:T(128)} %copy-done.9) | copy-start | bytes 772
  253.2 29.5 %copy-start.13 = (f32[1,64]{1,0:T(1,128)S(1)}, f32[1,64]{1,0:T(1,128)}, u32[]{:S(2)}) copy-start(f32[1,64]{1,0:T(1,128)} %param.20) | copy-start | bytes 772
  282.6 1.4 collective-permute-start.8
Sparse Core Ops, SparseCore 0:
  47.8 28.5 reduce-scatter.4
  113.9 26.8 reduce-scatter.6
  191.8 26.4 reduce-scatter.8
  254.7 26.8 reduce-scatter.10
where the time goes:
time: 292 us; the launch traced here: 291 us
  blocking collectives  127 us (43%)
  waiting for transfers between devices  114 us (39%)
  between operations  15 us (5%)
  other arithmetic  12.8 us (4%)
  matrix products  12.2 us (4%)
  local copies, waits for them, and re-layouts  6.03 us (2%)
  starting transfers between devices  4.77 us (2%)
    reduce_scatter x4, waiting for transfers between devices, reduce_rows(): lax.psum_scatter(jnp.dot(domain, weight, preferred_element_type=jnp.float...  108 us
    all_gather x4, blocking collectives, collect_rows(): lax.all_gather(values, 'tp', axis=0, tiled=True)  66.2 us
    all_gather x4, blocking collectives, collect_rows(): lax.all_gather(partner, 'tp', axis=0, tiled=True)  60.6 us
  transfers between devices with their start and end apart: 13, of which 9 were waited for; matrix products, arithmetic and copies ran while one was open for 1% of the time, Pallas kernels for 0%

commit v1 on v0

v1 whole, which is shorter than its diff:
```python
import functools

import jax
import jax.numpy as jnp
from jax import lax
from jax.experimental import pallas as pl
from jax.experimental.pallas import tpu as pltpu
from jax.sharding import PartitionSpec as P

MESH = pl.DeviceIdType.MESH
F32 = jnp.float32
BF16 = jnp.bfloat16
CHUNKS = 2


def flat(value):
    blocks, rows, columns = value.shape
    if rows % 16 == 0 or value.dtype == F32:
        return value.reshape(blocks * rows, columns)
    return value.astype(F32).reshape(blocks * rows, columns).astype(value.dtype)


def norm(values, gain):
    scaled = values * lax.rsqrt(jnp.mean(values * values, axis=-1, keepdims=True) + 1e-05)
    return (scaled * gain).astype(BF16)


def lifted(values):
    return jnp.maximum(values, 0.0) + jnp.exp(jnp.minimum(values, 0.0))


def kernel(
    n_layer,
    group,
    acts,
    fresh,
    gain_first,
    gain_second,
    w_qkv_hbm,
    w_out_hbm,
    w_gu_hbm,
    w_down_hbm,
    memory,
    totals,
    logit,
    first_out,
    second_out,
    memory_out,
    totals_out,
    w_qkv,
    w_out,
    w_gu,
    w_down,
    gathered,
    qkv,
    blended,
    hidden,
    given,
    taken,
    summed,
    arrived,
    stream,
    total,
    shifted,
    w_sem,
    ag_send,
    fw_send,
    ag_recv,
    x_send,
    x_recv,
    r_send,
    r_recv,
    sh_sem,
):
    place = lax.axis_index("layer")
    me = lax.axis_index("tp")
    half = lax.rem(place, 2)
    depth = lax.div(place, 2)
    base = half * group
    other_base = (1 - half) * group
    partner = (place + 1 - 2 * half, me)
    rows, width = acts.shape
    cols = width // CHUNKS
    head = memory.shape[-1]
    ff = w_down.shape[0]
    following = (lax.rem(place + 2, n_layer), me)
    previous = (lax.rem(place + n_layer - 2, n_layer), me)

    weights = [
        pltpu.make_async_copy(hbm, vmem, w_sem.at[k])
        for k, (hbm, vmem) in enumerate(
            [(w_qkv_hbm, w_qkv), (w_out_hbm, w_out), (w_gu_hbm, w_gu), (w_down_hbm, w_down)]
        )
    ]
    for copy in weights:
        copy.start()

    def peer(step):
        return lax.rem(me + step, group)

    barrier = pltpu.get_barrier_semaphore()
    for device in (partner, following, previous):
        pl.semaphore_signal(barrier, inc=1, device_id=device, device_id_type=MESH)

    def greet(step, _):
        pl.semaphore_signal(barrier, inc=1, device_id=(place, peer(step)), device_id_type=MESH)
        return 0

    lax.fori_loop(1, group, greet, 0)
    pl.semaphore_wait(barrier, 3 + group - 1)

    def block_copy(phase, slot, send_sem, device):
        return pltpu.make_async_remote_copy(
            src_ref=gathered.at[phase, slot],
            dst_ref=gathered.at[phase, slot],
            send_sem=send_sem,
            recv_sem=ag_recv.at[phase, slot],
            device_id=device,
            device_id_type=MESH,
        )

    def gather(phase, values, work):
        mine = base + me
        gathered[phase, mine] = values

        def send(step, _):
            target = peer(step)
            block_copy(phase, mine, ag_send.at[phase, target], (place, target)).start()
            return 0

        lax.fori_loop(1, group, send, 0)
        block_copy(phase, mine, ag_send.at[phase, me], partner).start()
        if phase < 2:
            weights[2 * phase].wait()
        work(mine)
        block_copy(phase, other_base + me, ag_send.at[phase, me], partner).wait_recv()
        work(other_base + me)

        def forward(step, _):
            source = peer(group - step)
            slot = base + source
            block_copy(phase, slot, ag_send.at[phase, me], partner).wait_recv()
            block_copy(phase, slot, fw_send.at[phase, source], partner).start()
            work(slot)
            return 0

        lax.fori_loop(1, group, forward, 0)

        def finish(step, _):
            slot = other_base + peer(group - step)
            block_copy(phase, slot, ag_send.at[phase, me], partner).wait_recv()
            work(slot)
            return 0

        lax.fori_loop(1, group, finish, 0)

    def exchange_copy(phase, chunk):
        part = pl.ds(chunk * cols, cols)
        return pltpu.make_async_remote_copy(
            src_ref=given.at[phase, :, :, part],
            dst_ref=taken.at[phase, :, :, part],
            send_sem=x_send.at[phase, chunk],
            recv_sem=x_recv.at[phase, chunk],
            device_id=partner,
            device_id_type=MESH,
        )

    def sum_copy(phase, chunk, target, source):
        part = pl.ds(chunk * cols, cols)
        return pltpu.make_async_remote_copy(
            src_ref=summed.at[phase, target, :, part],
            dst_ref=arrived.at[phase, source, :, part],
            send_sem=r_send.at[phase, chunk, target],
            recv_sem=r_recv.at[phase, chunk, source],
            device_id=(place, target),
            device_id_type=MESH,
        )

    def reduce(phase, local, weight, between):
        theirs = flat(local[pl.ds(other_base, group)])
        ours = flat(local[pl.ds(base, group)])
        for chunk in range(CHUNKS):
            part = slice(chunk * cols, (chunk + 1) * cols)
            term = jnp.dot(theirs, weight[:, part], preferred_element_type=F32)
            given[phase, :, :, part] = term.reshape(group, rows, cols).astype(BF16)
            exchange_copy(phase, chunk).start()
        for chunk in range(CHUNKS):
            part = slice(chunk * cols, (chunk + 1) * cols)
            term = jnp.dot(ours, weight[:, part], preferred_element_type=F32)
            exchange_copy(phase, chunk).wait_recv()
            term = term.reshape(group, rows, cols) + taken[phase, :, :, part].astype(F32)
            summed[phase, :, :, part] = term.astype(BF16)

            def send(step, _):
                sum_copy(phase, chunk, peer(step), me).start()
                return 0

            lax.fori_loop(1, group, send, 0)
        between()
        for chunk in range(CHUNKS):
            part = slice(chunk * cols, (chunk + 1) * cols)
            total[:, part] += summed[phase, me, :, part].astype(F32)

            def add(step, _):
                source = peer(group - step)
                sum_copy(phase, chunk, me, source).wait_recv()
                total[:, part] += arrived[phase, source, :, part].astype(F32)
                return 0

            lax.fori_loop(1, group, add, 0)

    def project(phase):
        def work(slot):
            qkv[slot] = jnp.dot(
                gathered[phase, slot], w_qkv[...], preferred_element_type=F32
            ).astype(BF16)

        return work

    def expand(phase):
        def work(slot):
            both = jnp.dot(gathered[phase, slot], w_gu[...], preferred_element_type=F32)
            gate = both[:, :ff]
            hidden[slot] = (gate / (1.0 + jnp.exp(-gate)) * both[:, ff:]).astype(BF16)

        return work

    def attend(memory_ref, totals_ref):
        all_rows = flat(qkv[...])
        seg = all_rows.shape[0]
        queries = all_rows[:, :head]
        keys = all_rows[:, head : 2 * head]
        values = all_rows[:, 2 * head :]
        scores = lax.dot_general(
            queries, keys, (((1,), (1,)), ((), ())), preferred_element_type=F32
        ) * head ** (-0.5)
        at_row = lax.broadcasted_iota(jnp.int32, (seg, seg), 0)
        at_col = lax.broadcasted_iota(jnp.int32, (seg, seg), 1)
        scores = jnp.where(at_row >= at_col, scores, -jnp.inf)
        powers = jnp.exp(scores - jnp.max(scores, axis=-1, keepdims=True))
        probs = (powers / jnp.sum(powers, axis=-1, keepdims=True)).astype(BF16)
        direct = jnp.dot(probs, values, preferred_element_type=F32)
        lifted_q = lifted(queries.astype(F32))
        numer = jnp.dot(
            lifted_q, memory_ref[...], preferred_element_type=F32, precision=lax.Precision.HIGHEST
        )
        denom = jnp.sum(lifted_q * totals_ref[...], axis=-1, keepdims=True)
        opened = 1.0 / (1.0 + jnp.exp(-logit[...]))
        mixed = opened * (numer / denom) + (1.0 - opened) * direct
        blended[...] = mixed.reshape(blended.shape).astype(BF16)

    def remember(memory_ref, totals_ref):
        all_rows = flat(qkv[...])
        lifted_k = lifted(all_rows[:, head : 2 * head].astype(F32))
        values = all_rows[:, 2 * head :].astype(F32)
        memory_out[...] = memory_ref[...] + lax.dot_general(
            lifted_k,
            values,
            (((0,), (0,)), ((), ())),
            preferred_element_type=F32,
            precision=lax.Precision.HIGHEST,
        )
        totals_out[...] = totals_ref[...] + jnp.sum(lifted_k, axis=0, keepdims=True)

    gain_one = gain_first[pl.ds(depth, 1), :]
    gain_two = gain_second[pl.ds(depth, 1), :]

    def layer(turn, memory_ref, totals_ref):
        first, second = 2 * turn, 2 * turn + 1
        start = stream[...].astype(F32)
        gather(first, norm(start, gain_one), project(first))
        total[...] = start
        attend(memory_ref, totals_ref)
        if turn == 0:
            weights[1].wait()
        reduce(first, blended, w_out, lambda: remember(memory_ref, totals_ref))
        middle = total[...].astype(BF16).astype(F32)
        gather_two = norm(middle, gain_two)
        total[...] = middle
        if turn == 0:
            gather(second, gather_two, expand(second))
            weights[3].wait()
        else:
            gather(second, gather_two, expand(second))
        reduce(second, hidden, w_down, lambda: None)

    stream[...] = acts[...]
    layer(0, memory, totals)
    first_out[...] = total[...].astype(BF16)
    relay = pltpu.make_async_remote_copy(
        src_ref=first_out,
        dst_ref=shifted,
        send_sem=sh_sem.at[0],
        recv_sem=sh_sem.at[1],
        device_id=following,
        device_id_type=MESH,
    )
    relay.start()
    relay.wait_recv()
    stream[...] = jnp.where(depth == 0, fresh[half].astype(F32), shifted[...].astype(F32)).astype(BF16)
    layer(1, memory_out, totals_out)
    second_out[...] = total[...].astype(BF16)

    relay.wait_send()
    for phase in range(4):
        block_copy(phase, base + me, ag_send.at[phase, me], partner).wait_send()
        for chunk in range(CHUNKS):
            exchange_copy(phase, chunk).wait_send()

        def drain(step, _):
            target = peer(step)
            block_copy(phase, base + me, ag_send.at[phase, target], partner).wait_send()
            block_copy(phase, base + target, fw_send.at[phase, target], partner).wait_send()
            for chunk in range(CHUNKS):
                sum_copy(phase, chunk, target, me).wait_send()
            return 0

        lax.fori_loop(1, group, drain, 0)


def solution(mesh):
    n_layer, group = mesh.shape["layer"], mesh.shape["tp"]

    def body(acts, fresh, g_one, g_two, p_qkv, p_out, p_gu, p_down, memory, totals, logits):
        rows, width = acts.shape
        head = memory.shape[-1]
        ff = p_down.shape[0]
        blocks = 2 * group
        gate_up = jnp.concatenate([p_gu[:, 0], p_gu[:, 1]], axis=1)
        vmem = pl.BlockSpec(memory_space=pltpu.VMEM)
        hbm = pl.BlockSpec(memory_space=pl.ANY)
        dma = pltpu.SemaphoreType.DMA
        outs = pl.pallas_call(
            functools.partial(kernel, n_layer, group),
            out_shape=(
                jax.ShapeDtypeStruct((rows, width), BF16),
                jax.ShapeDtypeStruct((rows, width), BF16),
                jax.ShapeDtypeStruct((head, head), F32),
                jax.ShapeDtypeStruct((1, head), F32),
            ),
            in_specs=[vmem] * 4 + [hbm] * 4 + [vmem] * 3,
            out_specs=(vmem,) * 4,
            scratch_shapes=[
                pltpu.VMEM((width, 3 * head), BF16),
                pltpu.VMEM((head, width), BF16),
                pltpu.VMEM((width, 2 * ff), BF16),
                pltpu.VMEM((ff, width), BF16),
                pltpu.VMEM((4, blocks, rows, width), BF16),
                pltpu.VMEM((blocks, rows, 3 * head), BF16),
                pltpu.VMEM((blocks, rows, head), BF16),
                pltpu.VMEM((blocks, rows, ff), BF16),
                pltpu.VMEM((4, group, rows, width), BF16),
                pltpu.VMEM((4, group, rows, width), BF16),
                pltpu.VMEM((4, group, rows, width), BF16),
                pltpu.VMEM((4, group, rows, width), BF16),
                pltpu.VMEM((rows, width), BF16),
                pltpu.VMEM((rows, width), F32),
                pltpu.VMEM((rows, width), BF16),
                dma((4,)),
                dma((4, group)),
                dma((4, group)),
                dma((4, blocks)),
                dma((4, CHUNKS)),
                dma((4, CHUNKS)),
                dma((4, CHUNKS, group)),
                dma((4, CHUNKS, group)),
                dma((2,)),
            ],
            compiler_params=pltpu.CompilerParams(
                collective_id=0, has_side_effects=True, vmem_limit_bytes=44 * 1024 * 1024
            ),
        )(
            acts,
            fresh,
            g_one,
            g_two,
            p_qkv[0],
            p_out,
            gate_up,
            p_down,
            memory[0],
            totals,
            logits[:, None],
        )
        return outs[0], outs[1], outs[2][None], outs[3]

    both = ("layer", "tp")
    in_specs = (
        P(both, None),
        P(None, "tp", None),
        P(),
        P(),
        P(both, None, None),
        P(both, None),
        P(None, None, both),
        P(both, None),
        P(both, None, None),
        P(both, None),
        P(both),
    )
    out_specs = (P(both, None), P(both, None), P(both, None, None), P(both, None))
    return jax.shard_map(body, mesh=mesh, in_specs=in_specs, out_specs=out_specs, check_vma=False)
```

time: 292 us -> 142 us (0.49)
  blocking collectives: 127 us -> 0 us
  Pallas kernels: 0 us -> 125 us
  waiting for transfers between devices: 114 us -> 0 us
  between operations: 15 us -> 1.37 us
  other arithmetic: 12.8 us -> 0.16 us
  matrix products: 12.2 us -> 0 us
  local copies, waits for them, and re-layouts: 6.03 us -> 14.5 us
  starting transfers between devices: 4.77 us -> 0 us
    all_gather x8 -> x0, blocking collectives: 127 us -> none  [the longest x4 66.2 us: collect_rows(): lax.all_gather(values, 'tp', axis=0, tiled=True)]
    pallas_call x0 -> x1, Pallas kernels: none -> 125 us  [body(): pl.pallas_call(functools.partial(kernel, n_layer, group), out_shape=(jax....]
    reduce_scatter x4 -> x0, waiting for transfers between devices: 108 us -> none  [reduce_rows(): lax.psum_scatter(jnp.dot(domain, weight, preferred_element_type=jnp.float...]
    dot_general x18 -> x0, matrix products: 12.2 us -> none  [the longest x4 5.56 us: reduce_rows(): jnp.dot(domain, weight, preferred_element_type=jnp.float32)]
    convert_element_type x16 -> x0, other arithmetic: 8.04 us -> none  [the longest x4 3.94 us: reduce_rows(): both = lax.psum_scatter(jnp.dot(domain, weight, preferred_element_type=jn...]
    unnamed x38 -> x21, local copies, waits for them, and re-layouts: 1.98 us -> 8.33 us
    slice x2 -> x1, local copies, waits for them, and re-layouts: 0.07 us -> 5.7 us  [body(): gate_up = jnp.concatenate([p_gu[:, 0], p_gu[:, 1]], axis=1)]
    ppermute x9 -> x0, waiting for transfers between devices: 5.45 us -> none  [the longest x8 4.39 us: partner_2(): return lax.ppermute(value, axis, pairs)]
  transfers between devices with their start and end apart: 13 -> 0, of which waited for: 9 -> 0; matrix products, arithmetic and copies ran while one was open for 1% -> 0% of each run, Pallas kernels for 0% -> 0%
where the time goes in v1:
time: 142 us; the launch traced here: 141 us
  Pallas kernels  125 us (88%)
  local copies, waits for them, and re-layouts  14.5 us (10%)
    pallas_call x1, Pallas kernels, body(): pl.pallas_call(functools.partial(kernel, n_layer, group), out_shape=(jax....  125 us
    unnamed x21, local copies, waits for them, and re-layouts  8.33 us
    slice x1, local copies, waits for them, and re-layouts, body(): gate_up = jnp.concatenate([p_gu[:, 0], p_gu[:, 1]], axis=1)  5.7 us

profile of v1, /device:TPU:0, one launch (start us, length us, event | category | flops | bytes accessed | tf_op | source)
XLA Modules:
  0.0 141.2 jit_solution(16672667884716378343)
XLA Ops:
  0.6 5.7 %fusion = (bf16[2048,1,256]{2,1,0:T(2,128)(2,1)S(1)}, bf16[2048,1,256]{2,1,0:T(2,128)(2,1)S(1)}) fusion(bf16[2048,2,256]{2,1,0:T(2,128)(2,1)} %param.17), kind=kLoop, calls=%fused_computation.3 | loop fusion | bytes 4194304 | tf_op jit(solution)/shard_map/slice | solution.py:329
  6.3 0.5 copy_bitcast_fusion
  6.8 0.0 copy-start.1
  6.8 0.0 copy-start.3
  6.8 0.0 copy-start.7
  6.8 0.2 pad_maximum_fusion.w_gu_hbm
  7.0 1.4 %copy.15 = bf16[1,2048,192]{2,1,0:T(8,128)(2,1)S(1)} copy(bf16[1,2048,192]{1,2,0:T(8,128)(2,1)} %param.15) | data formatting | bytes 1572864 | tf_op args[4]
  9.1 0.0 copy-done.1
  9.1 0.0 copy-done.3
  9.1 0.0 copy-done.7
  9.1 0.0 copy-start
  9.1 1.2 copy-done
  10.3 0.0 copy-start.2
  10.3 0.9 copy-done.2
  11.3 0.0 copy-start.4
  11.3 0.8 copy-done.4
  12.1 0.0 copy-start.5
  12.1 0.8 copy-done.5
  12.8 0.0 copy-start.6
  12.8 0.8 copy-done.6
  13.6 125.1 %shard_map.138 = (bf16[32,2048]{1,0:T(8,128)(2,1)S(1)}, bf16[32,2048]{1,0:T(8,128)(2,1)S(1)}, f32[64,64]{1,0:T(8,128)S(1)}, f32[1,64]{1,0:T(1,128)S(1)}) custom-call(bf16[32,2048]{1,0:T(8,128)(2,1)S(1)} %copy-done.3, bf16[2,32,2048]{2,1,0:T(8,128)(2,1)S(1)} %copy-done.1, f32[4,2048]{1,0:T(4,128)S(1)} %copy-done.4, f32[4,2048]{1,0:T(4,128)S(1)} %copy-done.5, ...), custom_call_target="tpu_custom_call" | custom-call | tf_op jit(solution)/shard_map/pallas_call | solution.py:333
  138.7 0.7 copy.27
  139.4 0.7 copy.28
  140.0 0.6 copy.29
  140.7 0.5 copy.30
Async XLA Ops:
  6.8 2.3 %copy-start.1 = (bf16[2,32,2048]{2,1,0:T(8,128)(2,1)S(1)}, bf16[2,32,2048]{2,1,0:T(8,128)(2,1)}, u32[]{:S(2)}) copy-start(bf16[2,32,2048]{2,1,0:T(8,128)(2,1)} %fresh.1) | copy-start | bytes 786436
  6.8 2.3 %copy-start.3 = (bf16[32,2048]{1,0:T(8,128)(2,1)S(1)}, bf16[32,2048]{1,0:T(8,128)(2,1)}, u32[]{:S(2)}) copy-start(bf16[32,2048]{1,0:T(8,128)(2,1)} %acts.1) | copy-start | bytes 393220
  6.8 2.3 %copy-start.7 = (f32[1,64]{1,0:T(1,128)S(1)}, f32[1,64]{1,0:T(1,128)}, u32[]{:S(2)}) copy-start(f32[1,64]{1,0:T(1,128)} %totals.1) | copy-start | bytes 772
  9.1 1.2 copy-start
  10.3 0.9 copy-start.2
  11.3 0.8 copy-start.4
  12.1 0.8 copy-start.5
  12.8 0.8 copy-start.6

commit v2 on v1

--- a/solution.py
+++ b/solution.py
@@ -32,25 +32,30 @@
 def kernel(
     n_layer,
     group,
-    acts,
-    fresh,
-    gain_first,
-    gain_second,
+    acts_hbm,
+    fresh_hbm,
+    gain_first_hbm,
+    gain_second_hbm,
     w_qkv_hbm,
     w_out_hbm,
     w_gu_hbm,
     w_down_hbm,
-    memory,
+    memory_hbm,
     totals,
     logit,
     first_out,
     second_out,
     memory_out,
     totals_out,
+    acts,
+    fresh,
+    gain_first,
+    gain_second,
     w_qkv,
     w_out,
     w_gu,
     w_down,
+    memory,
     gathered,
     qkv,
     blended,
@@ -59,6 +64,7 @@
     taken,
     summed,
     arrived,
+    relayed,
     stream,
     total,
     shifted,
@@ -70,6 +76,7 @@
     x_recv,
     r_send,
     r_recv,
+    l_recv,
     sh_sem,
 ):
     place = lax.axis_index("layer")
@@ -86,14 +93,28 @@
     following = (lax.rem(place + 2, n_layer), me)
     previous = (lax.rem(place + n_layer - 2, n_layer), me)
 
-    weights = [
+    loads = [
         pltpu.make_async_copy(hbm, vmem, w_sem.at[k])
         for k, (hbm, vmem) in enumerate(
-            [(w_qkv_hbm, w_qkv), (w_out_hbm, w_out), (w_gu_hbm, w_gu), (w_down_hbm, w_down)]
+            [
+                (acts_hbm, acts),
+                (gain_first_hbm, gain_first),
+                (w_qkv_hbm, w_qkv),
+                (memory_hbm, memory),
+                (w_out_hbm, w_out),
+                (gain_second_hbm, gain_second),
+                (w_gu_hbm, w_gu),
+                (w_down_hbm, w_down),
+                (fresh_hbm.at[half], fresh),
+            ]
         )
     ]
-    for copy in weights:
+    for copy in loads:
         copy.start()
+    near = me + 1 - 2 * lax.rem(me, 2)
+    mirror = group - 1 - me
+    opposite = lax.rem(me + 2, group)
+    inner = lax.rem(lax.div(me + 1, 2), 2)
 
     def peer(step):
         return lax.rem(me + step, group)
@@ -128,31 +149,61 @@
             block_copy(phase, mine, ag_send.at[phase, target], (place, target)).start()
             return 0
 
-        lax.fori_loop(1, group, send, 0)
+        def send_to(target):
+            block_copy(phase, mine, ag_send.at[phase, target], (place, target)).start()
+
+        if group == 4:
+            send_to(near + inner * (mirror - near))
+            send_to(mirror + inner * (near - mirror))
+
+            @pl.when(inner == 0)
+            def _():
+                send_to(opposite)
+        else:
+            lax.fori_loop(1, group, send, 0)
         block_copy(phase, mine, ag_send.at[phase, me], partner).start()
-        if phase < 2:
-            weights[2 * phase].wait()
+        if phase == 0:
+            loads[2].wait()
+        if phase == 1:
+            loads[6].wait()
         work(mine)
         block_copy(phase, other_base + me, ag_send.at[phase, me], partner).wait_recv()
         work(other_base + me)
 
+        order = [near + inner * (mirror - near), mirror + inner * (near - mirror), opposite]
+
         def forward(step, _):
-            source = peer(group - step)
+            source = order[step - 1] if group == 4 else peer(group - step)
             slot = base + source
             block_copy(phase, slot, ag_send.at[phase, me], partner).wait_recv()
+            if group == 4 and step == 1:
+
+                @pl.when(inner == 1)
+                def _():
+                    block_copy(phase, slot, ag_send.at[phase, opposite], (place, near)).start()
+
             block_copy(phase, slot, fw_send.at[phase, source], partner).start()
             work(slot)
             return 0
 
-        lax.fori_loop(1, group, forward, 0)
+        if group == 4:
+            for step in range(1, 4):
+                forward(step, 0)
+        else:
+            lax.fori_loop(1, group, forward, 0)
 
         def finish(step, _):
-            slot = other_base + peer(group - step)
+            source = order[step - 1] if group == 4 else peer(group - step)
+            slot = other_base + source
             block_copy(phase, slot, ag_send.at[phase, me], partner).wait_recv()
             work(slot)
             return 0
 
-        lax.fori_loop(1, group, finish, 0)
+        if group == 4:
+            for step in range(1, 4):
+                finish(step, 0)
+        else:
+            lax.fori_loop(1, group, finish, 0)
 
     def exchange_copy(phase, chunk):
         part = pl.ds(chunk * cols, cols)
@@ -173,6 +224,17 @@
             send_sem=r_send.at[phase, chunk, target],
             recv_sem=r_recv.at[phase, chunk, source],
             device_id=(place, target),
+            device_id_type=MESH,
+        )
+
+    def relay_copy(phase, chunk):
+        part = pl.ds(chunk * cols, cols)
+        return pltpu.make_async_remote_copy(
+            src_ref=summed.at[phase, opposite, :, part],
+            dst_ref=relayed.at[phase, :, part],
+            send_sem=r_send.at[phase, chunk, opposite],
+            recv_sem=l_recv.at[phase, chunk],
+            device_id=(place, near),
             device_id_type=MESH,
         )
 
@@ -195,7 +257,32 @@
                 sum_copy(phase, chunk, peer(step), me).start()
                 return 0
 
-            lax.fori_loop(1, group, send, 0)
+            if group == 4:
+
+                @pl.when(inner == 0)
+                def _():
+                    relay_copy(phase, chunk).start()
+                    sum_copy(phase, chunk, mirror, me).start()
+
+                @pl.when(inner == 1)
+                def _():
+                    sum_copy(phase, chunk, opposite, me).start()
+
+                sum_copy(phase, chunk, near, me).start()
+            else:
+                lax.fori_loop(1, group, send, 0)
+        if group == 4:
+
+            @pl.when(inner == 1)
+            def _():
+                for chunk in range(CHUNKS):
+                    part = slice(chunk * cols, (chunk + 1) * cols)
+                    relay_copy(phase, chunk).wait_recv()
+                    term = summed[phase, mirror, :, part].astype(F32)
+                    term += relayed[phase, :, part].astype(F32)
+                    summed[phase, mirror, :, part] = term.astype(BF16)
+                    sum_copy(phase, chunk, mirror, me).start()
+
         between()
         for chunk in range(CHUNKS):
             part = slice(chunk * cols, (chunk + 1) * cols)
@@ -207,21 +294,37 @@
                 total[:, part] += arrived[phase, source, :, part].astype(F32)
                 return 0
 
-            lax.fori_loop(1, group, add, 0)
+            def add_from(source):
+                sum_copy(phase, chunk, me, source).wait_recv()
+                total[:, part] += arrived[phase, source, :, part].astype(F32)
+
+            if group == 4:
+                add_from(near)
+                add_from(mirror)
+
+                @pl.when(inner == 0)
+                def _():
+                    add_from(opposite)
+            else:
+                lax.fori_loop(1, group, add, 0)
 
     def project(phase):
         def work(slot):
-            qkv[slot] = jnp.dot(
-                gathered[phase, slot], w_qkv[...], preferred_element_type=F32
+            qkv[slot] = lax.dot_general(
+                gathered[phase, slot],
+                w_qkv[...],
+                (((1,), (1,)), ((), ())),
+                preferred_element_type=F32,
             ).astype(BF16)
 
         return work
 
     def expand(phase):
         def work(slot):
-            both = jnp.dot(gathered[phase, slot], w_gu[...], preferred_element_type=F32)
-            gate = both[:, :ff]
-            hidden[slot] = (gate / (1.0 + jnp.exp(-gate)) * both[:, ff:]).astype(BF16)
+            row_block = gathered[phase, slot]
+            gate = jnp.dot(row_block, w_gu[:, 0].reshape(width, ff), preferred_element_type=F32)
+            up = jnp.dot(row_block, w_gu[:, 1].reshape(width, ff), preferred_element_type=F32)
+            hidden[slot] = (gate / (1.0 + jnp.exp(-gate)) * up).astype(BF16)
 
         return work
 
@@ -262,28 +365,30 @@
         )
         totals_out[...] = totals_ref[...] + jnp.sum(lifted_k, axis=0, keepdims=True)
 
-    gain_one = gain_first[pl.ds(depth, 1), :]
-    gain_two = gain_second[pl.ds(depth, 1), :]
-
     def layer(turn, memory_ref, totals_ref):
         first, second = 2 * turn, 2 * turn + 1
         start = stream[...].astype(F32)
-        gather(first, norm(start, gain_one), project(first))
+        gather(first, norm(start, gain_first[pl.ds(depth, 1), :]), project(first))
         total[...] = start
+        if turn == 0:
+            loads[3].wait()
         attend(memory_ref, totals_ref)
         if turn == 0:
-            weights[1].wait()
+            loads[4].wait()
+            loads[5].wait()
         reduce(first, blended, w_out, lambda: remember(memory_ref, totals_ref))
         middle = total[...].astype(BF16).astype(F32)
-        gather_two = norm(middle, gain_two)
+        gather_two = norm(middle, gain_second[pl.ds(depth, 1), :])
         total[...] = middle
         if turn == 0:
             gather(second, gather_two, expand(second))
-            weights[3].wait()
+            loads[7].wait()
         else:
             gather(second, gather_two, expand(second))
         reduce(second, hidden, w_down, lambda: None)
 
+    loads[0].wait()
+    loads[1].wait()
     stream[...] = acts[...]
     layer(0, memory, totals)
     first_out[...] = total[...].astype(BF16)
@@ -296,8 +401,9 @@
         device_id_type=MESH,
     )
     relay.start()
+    loads[8].wait()
     relay.wait_recv()
-    stream[...] = jnp.where(depth == 0, fresh[half].astype(F32), shifted[...].astype(F32)).astype(BF16)
+    stream[...] = jnp.where(depth == 0, fresh[...].astype(F32), shifted[...].astype(F32)).astype(BF16)
     layer(1, memory_out, totals_out)
     second_out[...] = total[...].astype(BF16)
 
@@ -318,6 +424,28 @@
         lax.fori_loop(1, group, drain, 0)
 
 
+def deliver(*refs):
+    sources, targets, sems = refs[:4], refs[4:8], refs[8]
+    copies = [
+        pltpu.make_async_copy(source, target, sems.at[k])
+        for k, (source, target) in enumerate(zip(sources, targets))
+    ]
+    for copy in copies:
+        copy.start()
+    for copy in copies:
+        copy.wait()
+
+
+def relaid(weight):
+    width, two, ff = weight.shape
+    block = 256
+    same = lax.broadcasted_iota(jnp.int32, (block, block), 0) == lax.broadcasted_iota(
+        jnp.int32, (block, block), 1
+    )
+    cut = weight.reshape(width // block, block, two, ff)
+    return jnp.einsum("bdtf,de->btef", cut, same.astype(BF16), preferred_element_type=BF16)
+
+
 def solution(mesh):
     n_layer, group = mesh.shape["layer"], mesh.shape["tp"]
 
@@ -326,7 +454,7 @@
         head = memory.shape[-1]
         ff = p_down.shape[0]
         blocks = 2 * group
-        gate_up = jnp.concatenate([p_gu[:, 0], p_gu[:, 1]], axis=1)
+        gate_up = relaid(p_gu)
         vmem = pl.BlockSpec(memory_space=pltpu.VMEM)
         hbm = pl.BlockSpec(memory_space=pl.ANY)
         dma = pltpu.SemaphoreType.DMA
@@ -338,13 +466,18 @@
                 jax.ShapeDtypeStruct((head, head), F32),
                 jax.ShapeDtypeStruct((1, head), F32),
             ),
-            in_specs=[vmem] * 4 + [hbm] * 4 + [vmem] * 3,
+            in_specs=[hbm] * 9 + [vmem] * 2,
             out_specs=(vmem,) * 4,
             scratch_shapes=[
-                pltpu.VMEM((width, 3 * head), BF16),
+                pltpu.VMEM((rows, width), BF16),
+                pltpu.VMEM((rows, width), BF16),
+                pltpu.VMEM(g_one.shape, F32),
+                pltpu.VMEM(g_two.shape, F32),
+                pltpu.VMEM((3 * head, width), BF16),
                 pltpu.VMEM((head, width), BF16),
-                pltpu.VMEM((width, 2 * ff), BF16),
+                pltpu.VMEM(gate_up.shape, BF16),
                 pltpu.VMEM((ff, width), BF16),
+                pltpu.VMEM((head, head), F32),
                 pltpu.VMEM((4, blocks, rows, width), BF16),
                 pltpu.VMEM((blocks, rows, 3 * head), BF16),
                 pltpu.VMEM((blocks, rows, head), BF16),
@@ -353,10 +486,11 @@
                 pltpu.VMEM((4, group, rows, width), BF16),
                 pltpu.VMEM((4, group, rows, width), BF16),
                 pltpu.VMEM((4, group, rows, width), BF16),
+                pltpu.VMEM((4, rows, width), BF16),
                 pltpu.VMEM((rows, width), BF16),
                 pltpu.VMEM((rows, width), F32),
                 pltpu.VMEM((rows, width), BF16),
-                dma((4,)),
+                dma((9,)),
                 dma((4, group)),
                 dma((4, group)),
                 dma((4, blocks)),
@@ -364,17 +498,18 @@
                 dma((4, CHUNKS)),
                 dma((4, CHUNKS, group)),
                 dma((4, CHUNKS, group)),
+                dma((4, CHUNKS)),
                 dma((2,)),
             ],
             compiler_params=pltpu.CompilerParams(
-                collective_id=0, has_side_effects=True, vmem_limit_bytes=44 * 1024 * 1024
+                collective_id=0, has_side_effects=True, vmem_limit_bytes=58 * 1024 * 1024
             ),
         )(
             acts,
             fresh,
             g_one,
             g_two,
-            p_qkv[0],
+            jnp.swapaxes(p_qkv[0], 0, 1),
             p_out,
             gate_up,
             p_down,
@@ -382,7 +517,14 @@
             totals,
             logits[:, None],
         )
-        return outs[0], outs[1], outs[2][None], outs[3]
+        first, second, after, norms = pl.pallas_call(
+            deliver,
+            out_shape=[jax.ShapeDtypeStruct(o.shape, o.dtype) for o in outs],
+            in_specs=[hbm] * 4,
+            out_specs=[hbm] * 4,
+            scratch_shapes=[dma((4,))],
+        )(*outs)
+        return first, second, after[None], norms
 
     both = ("layer", "tp")
     in_specs = (

time: 142 us -> 130 us (0.915)
  local copies, waits for them, and re-layouts: 14.5 us -> 0.81 us
  matrix products: 0 us -> 2.06 us
    pallas_call x0 -> x1, Pallas kernels: none -> 10.1 us  [body(): pl.pallas_call(deliver, out_shape=[jax.ShapeDtypeStruct(o.shape, o.dtype)...]
    pallas_call x1, Pallas kernels: 125 us -> 116 us  [body(): pl.pallas_call(functools.partial(kernel, n_layer, group), out_shape=(jax....]
    unnamed x21 -> x2, local copies, waits for them, and re-layouts: 8.33 us -> 0.81 us
    slice x1 -> x0, local copies, waits for them, and re-layouts: 5.7 us -> none  [body(): gate_up = jnp.concatenate([p_gu[:, 0], p_gu[:, 1]], axis=1)]
    dot_general x0 -> x1, matrix products: none -> 2.06 us  [relaid(): jnp.einsum('bdtf,de->btef', cut, same.astype(BF16), preferred_element_typ...]
where the time goes in v2:
time: 130 us
  Pallas kernels  126 us (97%)
  matrix products  2.06 us (2%)
  between operations  1.6 us (1%)
    pallas_call x1, Pallas kernels, body(): pl.pallas_call(functools.partial(kernel, n_layer, group), out_shape=(jax....  116 us
    pallas_call x1, Pallas kernels, body(): pl.pallas_call(deliver, out_shape=[jax.ShapeDtypeStruct(o.shape, o.dtype)...  10.1 us

profile of v2, /device:TPU:0, one launch (start us, length us, event | category | flops | bytes accessed | tf_op | source)
XLA Modules:
  0.0 130.1 jit_solution(7757965395885158942)
XLA Ops:
  0.6 0.0 copy-start
  1.4 0.8 copy-done
  2.2 2.1 %fusion.2.w_gu_hbm = bf16[8,2,256,256]{3,2,1,0:T(8,128)(2,1)} fusion(bf16[8,256,2,256]{3,2,1,0:T(2,128)(2,1)S(1)} %bitcast.15), kind=kOutput, calls=%fused_computation.2 | convolution fusion | flops 536936448 | bytes 4194304 | tf_op jit(solution)/shard_map/bdtf,de->btef/dot_general | solution.py:446
  4.3 115.5 %shard_map.138 = (bf16[32,2048]{1,0:T(8,128)(2,1)}, bf16[32,2048]{1,0:T(8,128)(2,1)}, f32[64,64]{1,0:T(8,128)}, f32[1,64]{1,0:T(1,128)}) custom-call(bf16[32,2048]{1,0:T(8,128)(2,1)} %acts_hbm.1, bf16[2,32,2048]{2,1,0:T(8,128)(2,1)} %fresh_hbm.1, f32[4,2048]{1,0:T(4,128)} %gain_first_hbm.1, f32[4,2048]{1,0:T(4,128)} %gain_second_hbm.1, ...), custom_call_target="tpu_custom_call" | custom-call | tf_op jit(solution)/shard_map/pallas_call | solution.py:461
  119.8 10.1 %shard_map.139 = (bf16[32,2048]{1,0:T(8,128)(2,1)}, bf16[32,2048]{1,0:T(8,128)(2,1)}, f32[64,64]{1,0:T(8,128)}, f32[1,64]{1,0:T(1,128)}) custom-call(bf16[32,2048]{1,0:T(8,128)(2,1)} %get-tuple-element.12.refs_0_, bf16[32,2048]{1,0:T(8,128)(2,1)} %get-tuple-element.13.refs_1_, f32[64,64]{1,0:T(8,128)} %get-tuple-element.14.refs_2_, ...), custom_call_target="tpu_custom_call" | custom-call | tf_op jit(solution)/shard_map/pallas_call | solution.py:520
Async XLA Ops:
  0.6 1.6 %copy-start = (bf16[2048,2,256]{2,1,0:T(2,128)(2,1)S(1)}, bf16[2048,2,256]{2,1,0:T(2,128)(2,1)}, u32[]{:S(2)}) copy-start(bf16[2048,2,256]{2,1,0:T(2,128)(2,1)} %param.17) | copy-start | bytes 6291460

commit v3 on v2

--- a/solution.py
+++ b/solution.py
@@ -77,6 +77,8 @@
     r_send,
     r_recv,
     l_recv,
+    e_send,
+    e_recv,
     sh_sem,
 ):
     place = lax.axis_index("layer")
@@ -140,7 +142,9 @@
             device_id_type=MESH,
         )
 
-    def gather(phase, values, work):
+    order = [near + inner * (mirror - near), mirror + inner * (near - mirror), opposite]
+
+    def announce(phase, values):
         mine = base + me
         gathered[phase, mine] = values
 
@@ -166,24 +170,28 @@
             loads[2].wait()
         if phase == 1:
             loads[6].wait()
-        work(mine)
+
+    def pass_on(phase, source, step):
+        slot = base + source
+        block_copy(phase, slot, ag_send.at[phase, me], partner).wait_recv()
+        if group == 4 and step == 1:
+
+            @pl.when(inner == 1)
+            def _():
+                block_copy(phase, slot, ag_send.at[phase, opposite], (place, near)).start()
+
+        block_copy(phase, slot, fw_send.at[phase, source], partner).start()
+
+    def gather(phase, values, work):
+        announce(phase, values)
+        work(base + me)
         block_copy(phase, other_base + me, ag_send.at[phase, me], partner).wait_recv()
         work(other_base + me)
 
-        order = [near + inner * (mirror - near), mirror + inner * (near - mirror), opposite]
-
         def forward(step, _):
             source = order[step - 1] if group == 4 else peer(group - step)
-            slot = base + source
-            block_copy(phase, slot, ag_send.at[phase, me], partner).wait_recv()
-            if group == 4 and step == 1:
-
-                @pl.when(inner == 1)
-                def _():
-                    block_copy(phase, slot, ag_send.at[phase, opposite], (place, near)).start()
-
-            block_copy(phase, slot, fw_send.at[phase, source], partner).start()
-            work(slot)
+            pass_on(phase, source, step)
+            work(base + source)
             return 0
 
         if group == 4:
@@ -327,6 +335,63 @@
             hidden[slot] = (gate / (1.0 + jnp.exp(-gate)) * up).astype(BF16)
 
         return work
+
+    def swap_copy(phase, source):
+        return pltpu.make_async_remote_copy(
+            src_ref=given.at[phase, source],
+            dst_ref=taken.at[phase, source],
+            send_sem=e_send.at[phase, source],
+            recv_sem=e_recv.at[phase, source],
+            device_id=partner,
+            device_id_type=MESH,
+        )
+
+    def whole_copy(phase, target, source):
+        return pltpu.make_async_remote_copy(
+            src_ref=summed.at[phase, target],
+            dst_ref=arrived.at[phase, source],
+            send_sem=r_send.at[phase, 0, target],
+            recv_sem=r_recv.at[phase, 0, source],
+            device_id=(place, target),
+            device_id_type=MESH,
+        )
+
+    def feed(phase, values):
+        work = expand(phase)
+        announce(phase, values)
+        work(base + me)
+        if phase == 1:
+            loads[7].wait()
+
+        def give(source):
+            slot = other_base + source
+            block_copy(phase, slot, ag_send.at[phase, me], partner).wait_recv()
+            work(slot)
+            term = jnp.dot(hidden[slot], w_down[...], preferred_element_type=F32)
+            given[phase, source] = term.astype(BF16)
+            swap_copy(phase, source).start()
+
+        def take(source):
+            term = jnp.dot(hidden[base + source], w_down[...], preferred_element_type=F32)
+            swap_copy(phase, source).wait_recv()
+            return term + taken[phase, source].astype(F32)
+
+        def give_back(source):
+            summed[phase, source] = take(source).astype(BF16)
+            whole_copy(phase, source, me).start()
+
+        give(me)
+        for step in range(1, 4):
+            pass_on(phase, order[step - 1], step)
+            work(base + order[step - 1])
+            if step > 1:
+                give_back(order[step - 2])
+            give(order[step - 1])
+        give_back(order[2])
+        total[...] += take(me)
+        for source in order:
+            whole_copy(phase, me, source).wait_recv()
+            total[...] += arrived[phase, source].astype(F32)
 
     def attend(memory_ref, totals_ref):
         all_rows = flat(qkv[...])
@@ -380,12 +445,13 @@
         middle = total[...].astype(BF16).astype(F32)
         gather_two = norm(middle, gain_second[pl.ds(depth, 1), :])
         total[...] = middle
-        if turn == 0:
-            gather(second, gather_two, expand(second))
-            loads[7].wait()
+        if group == 4:
+            feed(second, gather_two)
         else:
             gather(second, gather_two, expand(second))
-        reduce(second, hidden, w_down, lambda: None)
+            if turn == 0:
+                loads[7].wait()
+            reduce(second, hidden, w_down, lambda: None)
 
     loads[0].wait()
     loads[1].wait()
@@ -410,15 +476,23 @@
     relay.wait_send()
     for phase in range(4):
         block_copy(phase, base + me, ag_send.at[phase, me], partner).wait_send()
-        for chunk in range(CHUNKS):
-            exchange_copy(phase, chunk).wait_send()
+        piped = group == 4 and phase % 2 == 1
+        if piped:
+            swap_copy(phase, me).wait_send()
+        else:
+            for chunk in range(CHUNKS):
+                exchange_copy(phase, chunk).wait_send()
 
         def drain(step, _):
             target = peer(step)
             block_copy(phase, base + me, ag_send.at[phase, target], partner).wait_send()
             block_copy(phase, base + target, fw_send.at[phase, target], partner).wait_send()
-            for chunk in range(CHUNKS):
-                sum_copy(phase, chunk, target, me).wait_send()
+            if piped:
+                swap_copy(phase, target).wait_send()
+                whole_copy(phase, target, me).wait_send()
+            else:
+                for chunk in range(CHUNKS):
+                    sum_copy(phase, chunk, target, me).wait_send()
             return 0
 
         lax.fori_loop(1, group, drain, 0)
@@ -499,6 +573,8 @@
                 dma((4, CHUNKS, group)),
                 dma((4, CHUNKS, group)),
                 dma((4, CHUNKS)),
+                dma((4, group)),
+                dma((4, group)),
                 dma((2,)),
             ],
             compiler_params=pltpu.CompilerParams(
@@ -520,7 +596,7 @@
         first, second, after, norms = pl.pallas_call(
             deliver,
             out_shape=[jax.ShapeDtypeStruct(o.shape, o.dtype) for o in outs],
-            in_specs=[hbm] * 4,
+            in_specs=[vmem] * 4,
             out_specs=[hbm] * 4,
             scratch_shapes=[dma((4,))],
         )(*outs)

time: 130 us -> 119 us (0.915)
  Pallas kernels: 126 us -> 115 us
    pallas_call x1, Pallas kernels: 10.1 us -> 1.71 us  [body(): pl.pallas_call(deliver, out_shape=[jax.ShapeDtypeStruct(o.shape, o.dtype)...]
    pallas_call x1, Pallas kernels: 116 us -> 113 us  [body(): pl.pallas_call(functools.partial(kernel, n_layer, group), out_shape=(jax....]
where the time goes in v3:
time: 119 us
  Pallas kernels  115 us (97%)
  matrix products  2.06 us (2%)
  between operations  1.6 us (1%)
    pallas_call x1, Pallas kernels, body(): pl.pallas_call(functools.partial(kernel, n_layer, group), out_shape=(jax....  113 us

profile of v3, /device:TPU:0, one launch (start us, length us, event | category | flops | bytes accessed | tf_op | source)
XLA Modules:
  0.0 119.0 jit_solution(4431322150908535802)
XLA Ops:
  0.6 0.0 copy-start
  1.4 0.8 copy-done
  2.2 2.1 %fusion.2.w_gu_hbm = bf16[8,2,256,256]{3,2,1,0:T(8,128)(2,1)} fusion(bf16[8,256,2,256]{3,2,1,0:T(2,128)(2,1)S(1)} %bitcast.15), kind=kOutput, calls=%fused_computation.2 | convolution fusion | flops 536936448 | bytes 4194304 | tf_op jit(solution)/shard_map/bdtf,de->btef/dot_general | solution.py:520
  4.3 112.8 %shard_map.138 = (bf16[32,2048]{1,0:T(8,128)(2,1)}, bf16[32,2048]{1,0:T(8,128)(2,1)}, f32[64,64]{1,0:T(8,128)}, f32[1,64]{1,0:T(1,128)}) custom-call(bf16[32,2048]{1,0:T(8,128)(2,1)} %acts_hbm.1, bf16[2,32,2048]{2,1,0:T(8,128)(2,1)} %fresh_hbm.1, f32[4,2048]{1,0:T(4,128)} %gain_first_hbm.1, f32[4,2048]{1,0:T(4,128)} %gain_second_hbm.1, ...), custom_call_target="tpu_custom_call" | custom-call | tf_op jit(solution)/shard_map/pallas_call | solution.py:535
  117.1 1.7 %shard_map.139 = (bf16[32,2048]{1,0:T(8,128)(2,1)}, bf16[32,2048]{1,0:T(8,128)(2,1)}, f32[64,64]{1,0:T(8,128)}, f32[1,64]{1,0:T(1,128)}) custom-call(bf16[32,2048]{1,0:T(8,128)(2,1)} %get-tuple-element.12.refs_0_, bf16[32,2048]{1,0:T(8,128)(2,1)} %get-tuple-element.13.refs_1_, f32[64,64]{1,0:T(8,128)} %get-tuple-element.14.refs_2_, ...), custom_call_target="tpu_custom_call" | custom-call | tf_op jit(solution)/shard_map/pallas_call | solution.py:596
Async XLA Ops:
  0.6 1.6 %copy-start = (bf16[2048,2,256]{2,1,0:T(2,128)(2,1)S(1)}, bf16[2048,2,256]{2,1,0:T(2,128)(2,1)}, u32[]{:S(2)}) copy-start(bf16[2048,2,256]{2,1,0:T(2,128)(2,1)} %param.17) | copy-start | bytes 6291460

commit v4 on v3

--- a/solution.py
+++ b/solution.py
@@ -10,7 +10,7 @@
 MESH = pl.DeviceIdType.MESH
 F32 = jnp.float32
 BF16 = jnp.bfloat16
-CHUNKS = 2
+CHUNKS = 4
 
 
 def flat(value):

time: 119 us -> 125 us (1.050)
  Pallas kernels: 115 us -> 120 us
    pallas_call x1, Pallas kernels: 113 us -> 119 us  [body(): pl.pallas_call(functools.partial(kernel, n_layer, group), out_shape=(jax....]
where the time goes in v4:
time: 125 us
  Pallas kernels  120 us (96%)
  matrix products  2.06 us (2%)
  between operations  1.6 us (1%)
    pallas_call x1, Pallas kernels, body(): pl.pallas_call(functools.partial(kernel, n_layer, group), out_shape=(jax....  119 us

profile of v4, /device:TPU:0, one launch (start us, length us, event | category | flops | bytes accessed | tf_op | source)
XLA Modules:
  0.0 124.8 jit_solution(268249923368241297)
XLA Ops:
  0.6 0.0 copy-start
  1.4 0.8 copy-done
  2.2 2.1 %fusion.2.w_gu_hbm = bf16[8,2,256,256]{3,2,1,0:T(8,128)(2,1)} fusion(bf16[8,256,2,256]{3,2,1,0:T(2,128)(2,1)S(1)} %bitcast.15), kind=kOutput, calls=%fused_computation.2 | convolution fusion | flops 536936448 | bytes 4194304 | tf_op jit(solution)/shard_map/bdtf,de->btef/dot_general | solution.py:520
  4.3 118.6 %shard_map.138 = (bf16[32,2048]{1,0:T(8,128)(2,1)}, bf16[32,2048]{1,0:T(8,128)(2,1)}, f32[64,64]{1,0:T(8,128)}, f32[1,64]{1,0:T(1,128)}) custom-call(bf16[32,2048]{1,0:T(8,128)(2,1)} %acts_hbm.1, bf16[2,32,2048]{2,1,0:T(8,128)(2,1)} %fresh_hbm.1, f32[4,2048]{1,0:T(4,128)} %gain_first_hbm.1, f32[4,2048]{1,0:T(4,128)} %gain_second_hbm.1, ...), custom_call_target="tpu_custom_call" | custom-call | tf_op jit(solution)/shard_map/pallas_call | solution.py:535
  122.9 1.7 %shard_map.139 = (bf16[32,2048]{1,0:T(8,128)(2,1)}, bf16[32,2048]{1,0:T(8,128)(2,1)}, f32[64,64]{1,0:T(8,128)}, f32[1,64]{1,0:T(1,128)}) custom-call(bf16[32,2048]{1,0:T(8,128)(2,1)} %get-tuple-element.12.refs_0_, bf16[32,2048]{1,0:T(8,128)(2,1)} %get-tuple-element.13.refs_1_, f32[64,64]{1,0:T(8,128)} %get-tuple-element.14.refs_2_, ...), custom_call_target="tpu_custom_call" | custom-call | tf_op jit(solution)/shard_map/pallas_call | solution.py:596
Async XLA Ops:
  0.6 1.6 %copy-start = (bf16[2048,2,256]{2,1,0:T(2,128)(2,1)S(1)}, bf16[2048,2,256]{2,1,0:T(2,128)(2,1)}, u32[]{:S(2)}) copy-start(bf16[2048,2,256]{2,1,0:T(2,128)(2,1)} %param.17) | copy-start | bytes 6291460
